TPU v7x, 512 devices: a whole 4x8x8 slice. The times are simulated.
512 devices in a mesh: grp: 16 (over z, core), inner: 32 (over x, y).
Axes of the slice: x: 4, y: 8, z: 8, core: 2. Of those that a mesh axis runs over, the one named last changes fastest.
Arguments:
- queries: bfloat16 [256, 64, 192], P('inner', 'grp'), may hold values from -300 to 300
- tenant_ids: int32 [256], replicated, may hold values from 0 to 3
- prefix_lengths: int32 [4], replicated, may hold values from 2 to 4096, as said below
- latent_cache: bfloat16 [4096, 576], P('inner'), may hold values from -8 to 8
- key_absorb: bfloat16 [64, 128, 512], P('grp'), may hold values from -0.5 to 0.5
- value_absorb: bfloat16 [64, 512, 128], P('grp'), may hold values from -12 to 12
- key_down: bfloat16 [4, 64, 128, 16], P(None, 'grp'), may hold values from -0.5 to 0.5
- key_up: bfloat16 [4, 64, 16, 512], P(None, 'grp'), may hold values from -1.5 to 1.5
- value_down: bfloat16 [4, 64, 512, 16], P(None, 'grp'), may hold values from -6 to 6
- value_up: bfloat16 [4, 64, 16, 128], P(None, 'grp'), may hold values from -1.5 to 1.5
- out_proj: bfloat16 [8192, 7168], P('grp', 'inner'), may hold values from -0.0625 to 0.0625
Outputs:
- attended: bfloat16 [256, 7168], P('grp', 'inner')
Inputs may be any that keep to these rules, and one draw needn't show every extreme that they name: `prefix_lengths`: at least one tenant sees all 4096 positions.
All inputs are finite; a program needn't handle non-finite values.
Results may differ from a plain program's by a relative error of at most 0.011.
Values may be sent and summed in bfloat16 or wider, within the bound.
A program may use at most 64 MiB of HBM per device.

v0:
```python
import math

import jax
import jax.numpy as jnp
from jax import lax
from jax.sharding import PartitionSpec as P

LAT = 512
ROPE = 64
NOPE = 128


masked_score = -30000.0


def laid_out(parts, dim):
    parts = jnp.moveaxis(parts, 0, dim)
    dims = parts.shape
    return parts.reshape(*dims[:dim], dims[dim] * dims[dim + 1], *dims[dim + 2 :])


def sent_to_all(shard, axis):
    size = lax.axis_size(axis)
    return lax.all_to_all(
        jnp.broadcast_to(shard[None], (size, *shard.shape)), axis, 0, 0, tiled=True
    )


def gathered_copies(shard, axis, dim):
    return laid_out(sent_to_all(shard, axis), dim)


def of_everyone(shard, axis):
    everything = sent_to_all(shard, axis)
    return jnp.max(everything, axis=0)


def split_up(shard, dim, size):
    dims = shard.shape
    parts = shard.reshape(*dims[:dim], size, dims[dim] // size, *dims[dim + 1 :])
    return jnp.moveaxis(parts, dim, 0)


def sum_at_owner(shard, axis, dim):
    size = lax.axis_size(axis)
    parts = lax.all_to_all(split_up(shard, dim, size), axis, 0, 0, tiled=True)
    return jnp.sum(parts, axis=0)


def sent_together(arrays, axis, dim, along):
    widths = [math.prod(a.shape[along:]) for a in arrays]
    both = jnp.concatenate(
        [a.reshape(*a.shape[:along], w) for a, w in zip(arrays, widths)], axis=along
    )
    whole = sum_at_owner(both, axis, dim)
    parts = jnp.split(whole, [sum(widths[:k]) for k in range(1, len(widths))], axis=along)
    return tuple((b.reshape(*whole.shape[:along], *a.shape[along:]) for a, b in zip(arrays, parts)))


def absorb(queries, chosen, key_absorb, key_down, key_up):
    nope_part = queries[:, :, :NOPE]
    rope_part = queries[:, :, NOPE:]
    latent = jnp.einsum("thn,hnc->thc", nope_part, key_absorb, preferred_element_type=jnp.float32)
    lowrank = (
        jnp.einsum("thn,khnr->thkr", nope_part, key_down, preferred_element_type=jnp.float32)
        * chosen[:, None, :, None]
    )
    lowrank = lowrank.astype(jnp.bfloat16)
    latent = latent + jnp.einsum(
        "thkr,khrc->thc", lowrank, key_up, preferred_element_type=jnp.float32
    )
    return jnp.concatenate([latent, rope_part.astype(jnp.float32)], axis=2).astype(jnp.bfloat16)


def local(
    queries,
    tenant_ids,
    prefix_lengths,
    latent_cache,
    key_absorb,
    value_absorb,
    key_down,
    key_up,
    value_down,
    value_up,
    out_proj,
):
    tenant_count = prefix_lengths.shape[0]
    table = tenant_ids[:, None] == jnp.arange(tenant_count, dtype=jnp.int32)[None, :]
    chosen = table.astype(jnp.float32)
    limits = jnp.sum(jnp.where(table, prefix_lengths[None, :], 0), axis=1)
    gathered = gathered_copies(queries, "inner", 0)
    query_full = absorb(gathered, chosen, key_absorb, key_down, key_up)
    span = latent_cache.shape[0]
    scale = (NOPE + ROPE) ** (-0.5)
    scores = (
        jnp.einsum("thc,jc->thj", query_full, latent_cache, preferred_element_type=jnp.float32)
        * scale
    )
    positions = lax.axis_index("inner") * span + jnp.arange(span, dtype=jnp.int32)
    allowed = (positions[None, :] < limits[:, None])[:, None, :]
    masked = jnp.where(allowed, scores, masked_score)
    block_max = jnp.max(masked, axis=2)
    weights = jnp.where(allowed, jnp.exp(masked - block_max[:, :, None]), 0.0)
    block_sum = jnp.sum(weights, axis=2)
    block_latent = jnp.einsum(
        "thj,jc->thc",
        weights.astype(jnp.bfloat16),
        latent_cache[:, :LAT],
        preferred_element_type=jnp.float32,
    ).astype(jnp.bfloat16)
    values = jnp.einsum(
        "thc,hcv->thv", block_latent, value_absorb, preferred_element_type=jnp.float32
    )
    lowrank = (
        jnp.einsum("thc,khcr->thkr", block_latent, value_down, preferred_element_type=jnp.float32)
        * chosen[:, None, :, None]
    )
    lowrank = lowrank.astype(jnp.bfloat16)
    values = values + jnp.einsum(
        "thkr,khrv->thv", lowrank, value_up, preferred_element_type=jnp.float32
    )
    peak = of_everyone(block_max, "inner")
    factor = jnp.exp(block_max - peak)
    numer, denom = sent_together((values * factor[:, :, None], block_sum * factor), "inner", 0, 2)
    shares = (numer / denom[:, :, None]).astype(jnp.bfloat16)
    head_out = gathered_copies(shares, "inner", 0)
    total_rows = head_out.shape[0]
    flat = head_out.reshape(total_rows, head_out.shape[1] * head_out.shape[2])
    attended = sum_at_owner(jnp.dot(flat, out_proj, preferred_element_type=jnp.float32), "grp", 0)
    return attended.astype(jnp.bfloat16)


def solution(mesh):
    in_specs = (
        P("inner", "grp", None),
        P(),
        P(),
        P("inner", None),
        P("grp", None, None),
        P("grp", None, None),
        P(None, "grp", None, None),
        P(None, "grp", None, None),
        P(None, "grp", None, None),
        P(None, "grp", None, None),
        P("grp", "inner"),
    )
    out_specs = P("grp", "inner")
    return jax.shard_map(local, mesh=mesh, in_specs=in_specs, out_specs=out_specs, check_vma=False)
```

profile of v0, /device:TPU:1, one launch (start us, length us, event | category | flops | bytes accessed | tf_op | source)
XLA Modules:
  0.0 120.6 jit_solution(16049976777707092705)
XLA Ops:
  0.0 0.8 copy.41
  0.8 0.9 broadcast_in_dim.61
  1.6 10.5 %all-to-all-start = ((bf16[32,8,4,192]{3,1,2,0:T(8,128)(2,1)}), bf16[32,8,4,192]{3,1,2,0:T(8,128)(2,1)S(1)}, u32[]{:S(2)}, u32[]{:S(2)}) async-start(bf16[32,8,4,192]{3,1,2,0:T(8,128)(2,1)} %broadcast_in_dim.61), calls=%async_computation | async-start | bytes 1048576 | tf_op jit(solution)/shard_map/all_to_all | solution.py:24
  12.2 0.8 select_reduce_fusion
  12.9 0.7 fusion.40
  13.7 12.7 %all-to-all-done = bf16[32,8,4,192]{3,1,2,0:T(8,128)(2,1)S(1)} async-done(((bf16[32,8,4,192]{3,1,2,0:T(8,128)(2,1)}), bf16[32,8,4,192]{3,1,2,0:T(8,128)(2,1)S(1)}, u32[]{:S(2)}, u32[]{:S(2)}) %all-to-all-start) | async-done | bytes 393248 | tf_op jit(solution)/shard_map/all_to_all | solution.py:24
  26.6 0.1 copy.63
  26.7 1.5 %fusion.11 = f32[4,256,512,1]{1,2,3,0:T(8,128)S(1)} fusion(bf16[4,4,16,512]{3,2,1,0:T(8,128)(2,1)} %param.18, bf16[256,4,192]{2,0,1:T(8,128)(2,1)S(1)} %bitcast.66, f32[256,4]{0,1:T(4,128)S(1)} %fusion.40, bf16[4,4,128,16]{2,3,1,0:T(8,128)(2,1)S(1)} %copy-done.4), kind=kOutput, calls=%fused_computation.18 | convolution fusion | flops 84017152 | bytes 2691072 | tf_op jit(solution)/shard_map/thkr,khrc->thc/dot_general | solution.py:69
  28.3 0.5 fusion
  28.8 0.4 copy-done.3
  29.2 0.4 fusion.44
  29.6 0.7 broadcast_in_dim.64
  30.3 7.5 %all-to-all-start.1 = ((f32[32,256,4]{1,2,0:T(4,128)}), f32[32,256,4]{1,2,0:T(4,128)S(1)}, u32[]{:S(2)}, u32[]{:S(2)}) async-start(f32[32,256,4]{1,2,0:T(4,128)} %broadcast_in_dim.64), calls=%async_computation.1 | async-start | bytes 262144 | tf_op jit(solution)/shard_map/all_to_all | solution.py:24
  37.8 0.5 convolution_convert_fusion
  38.3 0.1 fusion.15
  38.4 1.6 %convolution_bitcast_fusion = f32[4,256,128]{2,1,0:T(8,128)S(1)} fusion(bf16[256,4,512]{2,0,1:T(8,128)(2,1)S(1)} %convolution_convert_fusion, bf16[4,4,512,16]{2,3,1,0:T(8,128)(2,1)} %param.19, f32[256,4]{0,1:T(4,128)S(1)} %fusion.40, bf16[4,4,16,128]{3,2,1,0:T(8,128)(2,1)S(1)} %copy-done.5), kind=kOutput, calls=%fused_computation.9 | convolution fusion | flops 84017152 | bytes 1904640 | tf_op jit(solution)/shard_map/thkr,khrv->thv/dot_general | solution.py:120
  40.0 6.9 %all-to-all-done.1 = f32[32,256,4]{1,2,0:T(4,128)S(1)} async-done(((f32[32,256,4]{1,2,0:T(4,128)}), f32[32,256,4]{1,2,0:T(4,128)S(1)}, u32[]{:S(2)}, u32[]{:S(2)}) %all-to-all-start.1) | async-done | bytes 131104 | tf_op jit(solution)/shard_map/all_to_all | solution.py:24
  47.1 0.8 copy.53
  47.9 0.4 fusion.4
  48.5 27.3 %all_to_all.25 = f32[32,8,4,129]{3,1,2,0:T(8,128)S(1)} all-to-all(f32[32,8,4,129]{3,1,2,0:T(8,128)S(1)} %pad_maximum_fusion), channel_id=1, replica_groups=mesh['grp'=16,'inner'=32] {'inner'}, dimensions={0} | all-to-all | bytes 1056768 | tf_op jit(solution)/shard_map/all_to_all | solution.py:46
  76.1 17.0 %all_to_all.26 = bf16[32,8,4,128]{3,1,2,0:T(8,128)(2,1)S(1)} all-to-all(bf16[32,8,4,128]{3,1,2,0:T(8,128)(2,1)S(1)} %broadcast_in_dim.65), channel_id=1, replica_groups=mesh['grp'=16,'inner'=32] {'inner'}, dimensions={0} | all-to-all | bytes 524288 | tf_op jit(solution)/shard_map/all_to_all | solution.py:24
  93.1 0.2 fusion.29
  93.3 26.6 %all_to_all.27 = f32[16,16,224]{2,1,0:T(8,128)S(1)} all-to-all(f32[16,16,224]{2,1,0:T(8,128)S(1)} %fusion.29), channel_id=1, replica_groups=mesh['grp'=16,'inner'=32] {'grp'}, dimensions={0} | all-to-all | bytes 458752 | tf_op jit(solution)/shard_map/all_to_all | solution.py:46
  120.0 0.6 reduce_sum.39
  (23 shorter events, 0.7 us)
Async XLA Ops:
  0.0 28.2 %copy-start = (bf16[4,128,512]{2,1,0:T(8,128)(2,1)S(1)}, bf16[4,128,512]{2,1,0:T(8,128)(2,1)}, u32[]{:S(2)}) copy-start(bf16[4,128,512]{2,1,0:T(8,128)(2,1)} %param.15) | copy-start | bytes 1572868
  0.0 26.7 %copy-start.4 = (bf16[4,4,128,16]{2,3,1,0:T(8,128)(2,1)S(1)}, bf16[4,4,128,16]{2,3,1,0:T(8,128)(2,1)}, u32[]{:S(2)}) copy-start(bf16[4,4,128,16]{2,3,1,0:T(8,128)(2,1)} %param.17) | copy-start | bytes 196612
  1.6 24.8 %all-to-all-start = ((bf16[32,8,4,192]{3,1,2,0:T(8,128)(2,1)}), bf16[32,8,4,192]{3,1,2,0:T(8,128)(2,1)S(1)}, u32[]{:S(2)}, u32[]{:S(2)}) async-start(bf16[32,8,4,192]{3,1,2,0:T(8,128)(2,1)} %broadcast_in_dim.61), calls=%async_computation | async-start | bytes 1048576 | tf_op jit(solution)/shard_map/all_to_all | solution.py:24
  28.2 0.9 copy-start.3
  29.6 8.8 %copy-start.5 = (bf16[4,4,16,128]{3,2,1,0:T(8,128)(2,1)S(1)}, bf16[4,4,16,128]{3,2,1,0:T(8,128)(2,1)}, u32[]{:S(2)}) copy-start(bf16[4,4,16,128]{3,2,1,0:T(8,128)(2,1)} %param.20) | copy-start | bytes 196612
  30.3 16.7 %all-to-all-start.1 = ((f32[32,256,4]{1,2,0:T(4,128)}), f32[32,256,4]{1,2,0:T(4,128)S(1)}, u32[]{:S(2)}, u32[]{:S(2)}) async-start(f32[32,256,4]{1,2,0:T(4,128)} %broadcast_in_dim.64), calls=%async_computation.1 | async-start | bytes 262144 | tf_op jit(solution)/shard_map/all_to_all | solution.py:24
  37.8 10.1 %copy-start.1 = (bf16[4,512,128]{2,1,0:T(8,128)(2,1)S(1)}, bf16[4,512,128]{2,1,0:T(8,128)(2,1)}, u32[]{:S(2)}) copy-start(bf16[4,512,128]{2,1,0:T(8,128)(2,1)} %param.16) | copy-start | bytes 1572868
  48.4 44.7 %copy-start.2 = (bf16[512,224]{0,1:T(8,128)(2,1)S(1)}, bf16[512,224]{0,1:T(8,128)(2,1)}, u32[]{:S(2)}) copy-start(bf16[512,224]{0,1:T(8,128)(2,1)} %param.21) | copy-start | bytes 688132
where the time goes:
time: 121 us
  blocking collectives  71 us (59%)
  waiting for transfers between devices  19.7 us (16%)
  starting transfers between devices  18 us (15%)
  matrix products  5.21 us (4%)
  local copies, waits for them, and re-layouts  3.98 us (3%)
  other arithmetic  2.58 us (2%)
    all_to_all x2, blocking collectives, sum_at_owner(): parts = lax.all_to_all(split_up(shard, dim, size), axis, 0, 0, tiled=True)  53.9 us
    all_to_all x2, waiting for transfers between devices, sent_to_all(): lax.all_to_all(jnp.broadcast_to(shard[None], (size, *shard.shape)), axis,...  19.7 us
    all_to_all x2, starting transfers between devices, sent_to_all(): lax.all_to_all(jnp.broadcast_to(shard[None], (size, *shard.shape)), axis,...  18 us
    all_to_all x1, blocking collectives, sent_to_all(): lax.all_to_all(jnp.broadcast_to(shard[None], (size, *shard.shape)), axis,...  17 us
  transfers between devices with their start and end apart: 2, of which 2 were waited for; matrix products, arithmetic and copies ran while one was open for 3% of the time, Pallas kernels for 0%

commit v1 on v0

v1 whole, which is shorter than its diff:
```python
import functools

import jax
import jax.numpy as jnp
from jax import lax
from jax.experimental import pallas as pl
from jax.experimental.pallas import tpu as pltpu
from jax.sharding import PartitionSpec as P

MESH = pl.DeviceIdType.MESH
BF, F32 = jnp.bfloat16, jnp.float32
LAT, ROPE, NOPE = 512, 64, 128
NX, NY, NG = 4, 8, 16
HEADS, TOK = 4, 8
SPAN = 128
MASKED = -30000.0
SCALE = (NOPE + ROPE) ** -0.5


def dot(a, b):
    return lax.dot_general(a, b, (((1,), (0,)), ((), ())), preferred_element_type=F32)


def dot_nt(a, b):
    return lax.dot_general(a, b, (((1,), (1,)), ((), ())), preferred_element_type=F32)


def kernel(
    q_hbm, ids_hbm, lim_hbm, lat_hbm, ka_hbm, va_hbm, kd_hbm, ku_hbm, vd_hbm, vu_hbm, wo_hbm,
    out_ref,
    q_v, q_n, q_r, ids_v, lim_s, lat, ka, va, kd, ku, vd, vu, wo,
    qbuf, qf, bl, vs, st, rv, rst, ho, zs, zr,
    lsem, q_ss, q_rs, l_ss, l_rs, v_ss, v_rs, s_ss, s_rs, y_ss, y_rs, x_ss, x_rs, z_ss, z_rs,
):
    g = lax.axis_index("grp")
    inner = lax.axis_index("inner")
    x, y = inner // NY, inner % NY

    def ypeer(d):
        return (y + d) % NY

    def xpeer(d):
        return (x + d) % NX

    def gpeer(d):
        return (g + d) % NG

    def remote(src, dst, ss, rs, to_g, to_inner):
        return pltpu.make_async_remote_copy(
            src_ref=src, dst_ref=dst, send_sem=ss, recv_sem=rs,
            device_id=(to_g, to_inner), device_id_type=MESH,
        )

    loads = {}
    for n, (name, src, dst) in enumerate((
        ("q", q_hbm, q_v), ("ids", ids_hbm, ids_v), ("lim", lim_hbm, lim_s), ("lat", lat_hbm, lat.at[x]),
        ("ka", ka_hbm, ka), ("kd", kd_hbm, kd), ("ku", ku_hbm, ku), ("va", va_hbm, va), ("vd", vd_hbm, vd),
        ("vu", vu_hbm, vu), ("wo", wo_hbm, wo),
    )):
        loads[name] = pltpu.make_async_copy(src, dst, lsem.at[n])
        loads[name].start()

    barrier = pltpu.get_barrier_semaphore()
    for d in range(1, NY):
        pl.semaphore_signal(barrier, 1, device_id=(g, x * NY + ypeer(d)), device_id_type=MESH)
    for d in range(1, NX):
        pl.semaphore_signal(barrier, 1, device_id=(g, xpeer(d) * NY + y), device_id_type=MESH)
    for d in range(1, NG):
        pl.semaphore_signal(barrier, 1, device_id=(gpeer(d), inner), device_id_type=MESH)

    loads["q"].wait()
    q32 = q_v[...].astype(F32)
    for t in range(TOK):
        q_n[t * HEADS : (t + 1) * HEADS, :] = q32[t, :, :NOPE]
        q_r[t * HEADS : (t + 1) * HEADS, :ROPE] = q32[t, :, NOPE:]
    rows = [q_n[pl.ds(h, TOK, stride=HEADS), :] for h in range(HEADS)]
    ropes = [q_r[pl.ds(h, TOK, stride=HEADS), :][:, :ROPE] for h in range(HEADS)]
    rows += [jnp.concatenate(ropes[h : h + 2], axis=1) for h in (0, 2)]
    qbuf[y] = jnp.concatenate(rows, axis=0).astype(BF)
    loads["lat"].wait()

    pl.semaphore_wait(barrier, NY - 1 + NX - 1 + NG - 1)

    sends = []
    order_y = (4, 3, 5, 2, 6, 1, 7)
    for d in order_y:
        sends.append(remote(qbuf.at[y], qbuf.at[y], q_ss.at[d], q_rs.at[y], g, x * NY + ypeer(d)))
        sends[-1].start()
    for d in (2, 1, 3):
        sends.append(remote(lat.at[x], lat.at[x], l_ss.at[d], l_rs.at[x], g, xpeer(d) * NY + y))
        sends[-1].start()

    loads["ids"].wait()
    loads["lim"].wait()
    span = NY * TOK
    wide = NX * span
    row = lax.broadcasted_iota(jnp.int32, (span, wide), 0)
    lane = lax.broadcasted_iota(jnp.int32, (span, wide), 1)
    tenant = jnp.sum(jnp.where(lane == row + x * span, ids_v[...], 0), axis=1, keepdims=True)
    limit = jnp.zeros_like(tenant)
    for k in range(4):
        limit = jnp.where(tenant == k, lim_s[k], limit)
    chosen = lax.broadcasted_iota(jnp.int32, (span, 64), 1) // 16 == tenant
    for name in ("ka", "kd", "ku", "va", "vd", "vu", "wo"):
        loads[name].wait()
    wo_all = jnp.concatenate([wo[...], jnp.zeros((32, LAT), BF)], axis=0)

    def arrived(dst, rs):
        remote(dst, dst, q_ss.at[0], rs, g, inner).wait_recv()

    for d in order_y:
        arrived(qbuf.at[ypeer(d)], q_rs.at[ypeer(d)])
    blocks = [qbuf[k].astype(F32) for k in range(NY)]
    half = lax.broadcasted_iota(jnp.int32, (span, NOPE), 1) // ROPE
    for h in range(HEADS):
        nope = jnp.concatenate([b[h * TOK : (h + 1) * TOK] for b in blocks], axis=0).astype(BF)
        first = HEADS * TOK + (h // 2) * TOK
        rope = jnp.concatenate([b[first : first + TOK] for b in blocks], axis=0)
        low = dot_nt(nope, kd[:, h].reshape(64, NOPE))
        low = jnp.where(chosen, low, 0.0).astype(BF)
        latent = dot(nope, ka[h]) + dot(low, ku[:, h].reshape(64, LAT))
        qf[h * span : (h + 1) * span, :LAT] = latent.astype(BF)
        qf[h * span : (h + 1) * span, LAT:] = jnp.where(half == h % 2, rope, 0.0).astype(BF)

    for d in (1, 3, 2):
        arrived(lat.at[xpeer(d)], l_rs.at[xpeer(d)])

    base = lax.broadcasted_iota(jnp.int32, (2 * span, SPAN), 1) + y * SPAN
    limit2 = jnp.concatenate([limit, limit], axis=0)
    eye = lax.broadcasted_iota(jnp.int32, (SPAN, SPAN), 0) == lax.broadcasted_iota(
        jnp.int32, (SPAN, SPAN), 1
    )
    for hp in range(2):
        mine = qf[hp * 2 * span : (hp + 1) * 2 * span, :]
        scores, okay = [], []
        for b in range(NX):
            keys = jnp.concatenate([lat[b], lat[b, LAT:]], axis=0)
            okay.append(base + b * NY * SPAN < limit2)
            scores.append(jnp.where(okay[b], dot(mine, keys) * SCALE, MASKED))
        top = functools.reduce(jnp.maximum, scores)
        top = jnp.max(top, axis=1, keepdims=True)
        weights = [jnp.where(ok, jnp.exp(s - top), 0.0) for ok, s in zip(okay, scores)]
        total = jnp.sum(functools.reduce(jnp.add, weights), axis=1, keepdims=True)
        acc = functools.reduce(
            jnp.add, [dot_nt(w.astype(BF), lat[b, :LAT]) for b, w in enumerate(weights)]
        )
        bl[...] = acc.astype(BF)
        st[hp, 0:1, :] = jnp.sum(jnp.where(eye, top, 0.0), axis=0, keepdims=True)
        st[hp, 1:2, :] = jnp.sum(jnp.where(eye, total, 0.0), axis=0, keepdims=True)
        for hl in range(2):
            h = hp * 2 + hl
            mine = bl[hl * span : (hl + 1) * span, :]
            low = dot_nt(mine, vd[:, h].reshape(64, LAT))
            low = jnp.where(chosen, low, 0.0).astype(BF)
            values = (dot(mine, va[h]) + dot(low, vu[:, h].reshape(64, NOPE))).astype(BF)
            for tb in range(4):
                vs[tb * 2 + hp, hl * 16 : (hl + 1) * 16, :] = values[tb * 16 : (tb + 1) * 16]

    for d in order_y:
        to = ypeer(d)
        sends.append(remote(vs.at[to], rv.at[y], v_ss.at[d], v_rs.at[y], g, x * NY + to))
        sends[-1].start()
        sends.append(remote(st.at[to % 2], rst.at[y], s_ss.at[d], s_rs.at[y], g, x * NY + to))
        sends[-1].start()
    rv[y] = vs[y]
    rst[y] = st[y % 2]
    for d in order_y:
        arrived(rst.at[ypeer(d)], s_rs.at[ypeer(d)])

    tops = [rst[k, 0:1, :] for k in range(NY)]
    peak = functools.reduce(jnp.maximum, tops)
    factors = [jnp.exp(t - peak) for t in tops]
    denom = functools.reduce(jnp.add, [f * rst[k, 1:2, :] for k, f in enumerate(factors)])
    r32 = lax.broadcasted_iota(jnp.int32, (32, SPAN), 0)
    l32 = lax.broadcasted_iota(jnp.int32, (32, SPAN), 1)
    pick = l32 == (r32 // 16) * span + (y // 2) * 16 + r32 % 16
    shares = [
        jnp.sum(jnp.where(pick, f / denom, 0.0), axis=1, keepdims=True) for f in factors
    ]
    for d in order_y:
        arrived(rv.at[ypeer(d)], v_rs.at[ypeer(d)])
    head = functools.reduce(jnp.add, [s * rv[k].astype(F32) for k, s in enumerate(shares)])
    ho[x, y] = jnp.concatenate([head[:16], head[16:]], axis=1).astype(BF)

    for d in order_y:
        sends.append(
            remote(ho.at[x, y], ho.at[x, y], y_ss.at[d], y_rs.at[y], g, x * NY + ypeer(d))
        )
        sends[-1].start()
    for d in order_y:
        arrived(ho.at[x, ypeer(d)], y_rs.at[ypeer(d)])
    for d in (2, 1, 3):
        sends.append(remote(ho.at[x], ho.at[x], x_ss.at[d], x_rs.at[x], g, xpeer(d) * NY + y))
        sends[-1].start()

    for e in (0, 1, 3, 2):
        xx = xpeer(e)
        if e:
            arrived(ho.at[xx], x_rs.at[xx])
        lhs = jnp.concatenate(
            [
                jnp.concatenate([ho[xx, 2 * tb], ho[xx, 2 * tb + 1]], axis=1)
                for tb in range(4)
            ],
            axis=0,
        )
        part = dot_nt(lhs, wo_all).astype(BF)
        for tb in range(4):
            zs[4 * xx + tb] = part[tb * 16 : (tb + 1) * 16]
    for d in (8, 9, 7, 6, 10, 5, 11, 4, 12, 3, 13, 2, 14, 15, 1):
        to = gpeer(d)
        sends.append(remote(zs.at[to], zr.at[g], z_ss.at[d], z_rs.at[g], to, inner))
        sends[-1].start()
    zr[g] = zs[g]
    for d in range(1, NG):
        arrived(zr.at[gpeer(d)], z_rs.at[gpeer(d)])
    whole = functools.reduce(jnp.add, [zr[k].astype(F32) for k in range(NG)])
    out_ref[...] = whole[:, : out_ref.shape[1]].astype(BF)
    for s in sends:
        s.wait_send()


def local(q, ids, limits, latent, ka, va, kd, ku, vd, vu, wo):
    args = (
        q, ids.reshape(1, -1), limits, latent.T, ka, va, kd.swapaxes(2, 3), ku,
        vd.swapaxes(2, 3), vu, wo.T,
    )
    sem = pltpu.SemaphoreType.DMA
    v = pltpu.VMEM
    return pl.pallas_call(
        kernel,
        out_shape=jax.ShapeDtypeStruct((q.shape[0] * 2, wo.shape[1]), BF),
        in_specs=[pl.BlockSpec(memory_space=pltpu.HBM)] * len(args),
        out_specs=pl.BlockSpec(memory_space=pltpu.VMEM),
        scratch_shapes=[
            v(q.shape, BF),
            v((TOK * HEADS, NOPE), F32),
            v((TOK * HEADS, NOPE), F32),
            v((1, ids.shape[0]), jnp.int32),
            pltpu.SMEM(limits.shape, jnp.int32),
            v((NX, LAT + ROPE, SPAN), BF),
            v(ka.shape, BF),
            v(va.shape, BF),
            v(args[6].shape, BF),
            v(ku.shape, BF),
            v(args[8].shape, BF),
            v(vu.shape, BF),
            v(args[10].shape, BF),
            v((NY, 48, 128), BF),
            v((HEADS * NY * TOK, LAT + 128), BF),
            v((2 * NY * TOK, LAT), BF),
            v((NY, 32, 128), BF),
            v((2, 8, 128), F32),
            v((NY, 32, 128), BF),
            v((NY, 8, 128), F32),
            v((NX, NY, 16, 256), BF),
            v((NG, 16, 256), BF),
            v((NG, 16, 256), BF),
            sem((len(args),)),
            *[sem((NY,))] * 2,
            *[sem((NX,))] * 2,
            *[sem((NY,))] * 6,
            *[sem((NX,))] * 2,
            *[sem((NG,))] * 2,
        ],
        compiler_params=pltpu.CompilerParams(
            collective_id=0, has_side_effects=True
        ),
    )(*args)


def solution(mesh):
    in_specs = (
        P("inner", "grp", None),
        P(),
        P(),
        P("inner", None),
        P("grp", None, None),
        P("grp", None, None),
        P(None, "grp", None, None),
        P(None, "grp", None, None),
        P(None, "grp", None, None),
        P(None, "grp", None, None),
        P("grp", "inner"),
    )
    return jax.shard_map(
        local, mesh=mesh, in_specs=in_specs, out_specs=P("grp", "inner"), check_vma=False
    )
```

time: 121 us -> 47.6 us (0.39)
  blocking collectives: 71 us -> 0 us
  Pallas kernels: 0 us -> 46.1 us
  waiting for transfers between devices: 19.7 us -> 0 us
  starting transfers between devices: 18 us -> 0 us
  matrix products: 5.21 us -> 0 us
  local copies, waits for them, and re-layouts: 3.98 us -> 1.3 us
  other arithmetic: 2.58 us -> 0 us
    all_to_all x3 -> x0, blocking collectives: 71 us -> none  [the longest x2 53.9 us: sum_at_owner(): parts = lax.all_to_all(split_up(shard, dim, size), axis, 0, 0, tiled=True)]
    pallas_call x0 -> x1, Pallas kernels: none -> 46.1 us  [local(): pl.pallas_call(kernel, out_shape=jax.ShapeDtypeStruct((q.shape[0] * 2, wo...]
    all_to_all x2 -> x0, waiting for transfers between devices: 19.7 us -> none  [sent_to_all(): lax.all_to_all(jnp.broadcast_to(shard[None], (size, *shard.shape)), axis,...]
    all_to_all x2 -> x0, starting transfers between devices: 18 us -> none  [sent_to_all(): lax.all_to_all(jnp.broadcast_to(shard[None], (size, *shard.shape)), axis,...]
    dot_general x7 -> x0, matrix products: 5.21 us -> none  [the longest x1 1.61 us: local(): jnp.einsum('thkr,khrv->thv', lowrank, value_up, preferred_element_type=jn...]
    reduce_sum x4 -> x0, other arithmetic: 1.6 us -> none  [the longest x1 0.78 us: local(): limits = jnp.sum(jnp.where(table, prefix_lengths[None, :], 0), axis=1)]
    broadcast_in_dim x3 -> x0, local copies, waits for them, and re-layouts: 1.54 us -> none  [sent_to_all(): jnp.broadcast_to(shard[None], (size, *shard.shape))]
  transfers between devices with their start and end apart: 2 -> 0, of which waited for: 2 -> 0; matrix products, arithmetic and copies ran while one was open for 3% -> 0% of each run, Pallas kernels for 0% -> 0%
where the time goes in v1:
time: 47.6 us; the launch traced here: 47.4 us
  Pallas kernels  46.1 us (97%)
  local copies, waits for them, and re-layouts  1.3 us (3%)
    pallas_call x1, Pallas kernels, local(): pl.pallas_call(kernel, out_shape=jax.ShapeDtypeStruct((q.shape[0] * 2, wo...  46.1 us
    unnamed x1, local copies, waits for them, and re-layouts  1.3 us

profile of v1, /device:TPU:1, one launch (start us, length us, event | category | flops | bytes accessed | tf_op | source)
XLA Modules:
  0.0 47.4 jit_solution(8358465742307353173)
XLA Ops:
  0.0 46.1 %shard_map.109 = bf16[16,224]{1,0:T(8,128)(2,1)} custom-call(bf16[8,4,192]{2,1,0:T(4,128)(2,1)} %q_hbm.1, s32[1,256]{1,0:T(1,128)} %bitcast.9, s32[4]{0:T(128)} %lim_hbm.1, bf16[576,128]{1,0:T(8,128)(2,1)} %bitcast.7, bf16[4,128,512]{2,1,0:T(8,128)(2,1)} %ka_hbm.1, bf16[4,512,128]{2,1,0:T(8,128)(2,1)} %va_hbm.1, bf16[4,4,16,128]{3,2,1,0:T(8,128)(2,1)} %bitcast.8, ...), custom_call_target="tpu_custom_call" | custom-call | tf_op jit(solution)/shard_map/pallas_call | solution.py:230
  46.1 1.3 %copy.13 = bf16[16,224]{1,0:T(8,128)(2,1)} copy(bf16[16,224]{1,0:T(8,128)(2,1)} %shard_map.109) | data formatting | bytes 14336

commit v2 on v1

v2 whole, which is shorter than its diff:
```python
import functools

import jax
import jax.numpy as jnp
from jax import lax
from jax.experimental import pallas as pl
from jax.experimental.pallas import tpu as pltpu
from jax.sharding import PartitionSpec as P

MESH = pl.DeviceIdType.MESH
BF, F32 = jnp.bfloat16, jnp.float32
LAT, ROPE, NOPE = 512, 64, 128
NX, NY, NG = 4, 8, 16
HEADS, TOK = 4, 8
SPAN = 128
MASKED = -30000.0
FAR_Y, FAR_X = (4, 3, 5, 2, 6, 1, 7), (2, 1, 3)
SCALE = (NOPE + ROPE) ** -0.5


def dot(a, b):
    return lax.dot_general(a, b, (((1,), (0,)), ((), ())), preferred_element_type=F32)


def dot_nt(a, b):
    return lax.dot_general(a, b, (((1,), (1,)), ((), ())), preferred_element_type=F32)


def kernel(
    q_hbm, ids_hbm, lim_hbm, lat_hbm, ka_hbm, va_hbm, kd_hbm, ku_hbm, vd_hbm, vu_hbm, wo_hbm,
    z_out,
    q_v, q_n, q_r, ids_v, lim_s, lat, ka, va, kd, ku, vd, vu, wo,
    qbuf, qf, vs, rv, ho, zs,
    lsem, q_ss, q_rs, l_ss, l_rs, c_ss, c_rs, v_ss, v_rs, y_ss, y_rs, x_ss, x_rs, z_ss, z_rs,
):
    g = lax.axis_index("grp")
    inner = lax.axis_index("inner")
    x, y = inner // NY, inner % NY

    def ypeer(d):
        return (y + d) % NY

    def xpeer(d):
        return (x + d) % NX

    def gpeer(d):
        return (g + d) % NG

    def remote(src, dst, ss, rs, to_g, to_inner):
        return pltpu.make_async_remote_copy(
            src_ref=src, dst_ref=dst, send_sem=ss, recv_sem=rs,
            device_id=(to_g, to_inner), device_id_type=MESH,
        )

    def load(n, src, dst):
        copy = pltpu.make_async_copy(src, dst, lsem.at[n])
        copy.start()
        return copy

    def arrived(dst, rs):
        remote(dst, dst, q_ss.at[0], rs, g, inner).wait_recv()

    sends = []

    def send(*what):
        copy = remote(*what)
        copy.start()
        sends.append(copy)

    get_q = load(0, q_hbm, q_v)
    get_lat = load(1, lat_hbm, lat.at[x])
    barrier = pltpu.get_barrier_semaphore()
    for d in FAR_Y:
        pl.semaphore_signal(barrier, 1, device_id=(g, x * NY + ypeer(d)), device_id_type=MESH)
    for d in FAR_X:
        pl.semaphore_signal(barrier, 1, device_id=(g, xpeer(d) * NY + y), device_id_type=MESH)
    for d in range(1, NG):
        pl.semaphore_signal(barrier, 1, device_id=(gpeer(d), inner), device_id_type=MESH)

    get_q.wait()
    q32 = q_v[...].astype(F32)
    for t in range(TOK):
        q_n[t * HEADS : (t + 1) * HEADS, :] = q32[t, :, :NOPE]
        q_r[t * HEADS : (t + 1) * HEADS, :ROPE] = q32[t, :, NOPE:]
    rows = [q_n[pl.ds(h, TOK, stride=HEADS), :] for h in range(HEADS)]
    ropes = [q_r[pl.ds(h, TOK, stride=HEADS), :][:, :ROPE] for h in range(HEADS)]
    rows += [jnp.concatenate(ropes[h : h + 2], axis=1) for h in (0, 2)]
    qbuf[y] = jnp.concatenate(rows, axis=0).astype(BF)
    get_lat.wait()

    pl.semaphore_wait(barrier, NY - 1 + NX - 1 + NG - 1)

    for d in FAR_Y:
        send(qbuf.at[y], qbuf.at[y], q_ss.at[d], q_rs.at[y], g, x * NY + ypeer(d))
    part = pl.ds(pl.multiple_of((g % 2) * 288, 16), 288)
    for d in FAR_X:
        piece = lat.at[x, part]
        send(piece, piece, l_ss.at[d], l_rs.at[x], g, xpeer(d) * NY + y)
    get = [
        load(n + 2, src, dst)
        for n, (src, dst) in enumerate((
            (ids_hbm, ids_v), (lim_hbm, lim_s), (ka_hbm, ka), (kd_hbm, kd), (ku_hbm, ku), (va_hbm, va),
            (vd_hbm, vd), (vu_hbm, vu), (wo_hbm, wo.at[: wo_hbm.shape[0]]),
        ))
    ]

    wo[wo_hbm.shape[0] :, :] = jnp.zeros((wo.shape[0] - wo_hbm.shape[0], LAT), BF)
    for copy in get:
        copy.wait()
    span = NY * TOK
    wide = NX * span
    row = lax.broadcasted_iota(jnp.int32, (span, wide), 0)
    lane = lax.broadcasted_iota(jnp.int32, (span, wide), 1)
    tenant = jnp.sum(jnp.where(lane == row + x * span, ids_v[...], 0), axis=1, keepdims=True)
    limit = jnp.zeros_like(tenant)
    for k in range(4):
        limit = jnp.where(tenant == k, lim_s[k], limit)
    chosen = lax.broadcasted_iota(jnp.int32, (span, 64), 1) // 16 == tenant

    for d in FAR_Y:
        arrived(qbuf.at[ypeer(d)], q_rs.at[ypeer(d)])
    core = g + 1 - 2 * (g % 2)
    for d in (1, 3, 2):
        piece = lat.at[xpeer(d), part]
        arrived(piece, l_rs.at[xpeer(d)])
        send(piece, piece, c_ss.at[d], c_rs.at[d], core, inner)

    blocks = [qbuf[k].astype(F32) for k in range(NY)]
    half = lax.broadcasted_iota(jnp.int32, (span, NOPE), 1) // ROPE
    for h in range(HEADS):
        nope = jnp.concatenate([b[h * TOK : (h + 1) * TOK] for b in blocks], axis=0).astype(BF)
        first = HEADS * TOK + (h // 2) * TOK
        rope = jnp.concatenate([b[first : first + TOK] for b in blocks], axis=0)
        low = dot_nt(nope, kd[:, h].reshape(64, NOPE))
        low = jnp.where(chosen, low, 0.0).astype(BF)
        latent = dot(nope, ka[h]) + dot(low, ku[:, h].reshape(64, LAT))
        rows = pl.ds((h % 2) * span, span)
        qf[h // 2, rows, :LAT] = latent.astype(BF)
        qf[h // 2, rows, LAT:] = jnp.where(half == h % 2, rope, 0.0).astype(BF)

    other = pl.ds(pl.multiple_of((1 - g % 2) * 288, 16), 288)
    for d in (1, 3, 2):
        arrived(lat.at[xpeer(d), other], c_rs.at[d])

    base = lax.broadcasted_iota(jnp.int32, (2 * span, SPAN), 1) + y * SPAN
    limit2 = jnp.concatenate([limit, limit], axis=0)
    eye = lax.broadcasted_iota(jnp.int32, (SPAN, SPAN), 0) == lax.broadcasted_iota(
        jnp.int32, (SPAN, SPAN), 1
    )
    okay = [base + b * NY * SPAN < limit2 for b in range(NX)]
    for turn, peers in enumerate(((4, 2, 6, 0), (3, 5, 1, 7))):
        hp = (y + turn) % 2
        mine = qf[hp]
        scores = []
        for b in range(NX):
            keys = jnp.concatenate([lat[b], lat[b, LAT:]], axis=0)
            scores.append(jnp.where(okay[b], dot(mine, keys) * SCALE, MASKED))
        top = functools.reduce(jnp.maximum, scores)
        top = jnp.max(top, axis=1, keepdims=True)
        weights = [jnp.where(ok, jnp.exp(s - top), 0.0) for ok, s in zip(okay, scores)]
        total = jnp.sum(functools.reduce(jnp.add, weights), axis=1, keepdims=True)
        acc = functools.reduce(
            jnp.add, [dot_nt(w.astype(BF), lat[b, :LAT]) for b, w in enumerate(weights)]
        ).astype(BF)
        three = []
        for column in (top, total):
            rest = jnp.sum(jnp.where(eye, column, 0.0), axis=0, keepdims=True)
            for _ in range(3):
                three.append(rest.astype(BF).astype(F32))
                rest = rest - three[-1]
        three = jnp.concatenate(three + [jnp.zeros((10, SPAN), F32)], axis=0).astype(BF)
        values = []
        for hl in range(2):
            h = hp * 2 + hl
            mine = acc[hl * span : (hl + 1) * span, :]
            low = dot_nt(mine, vd[:, h].reshape(64, LAT))
            low = jnp.where(chosen, low, 0.0).astype(BF)
            values.append((dot(mine, va[h]) + dot(low, vu[:, h].reshape(64, NOPE))).astype(BF))
        for tb in range(4):
            vs[tb * 2 + hp] = jnp.concatenate(
                [values[0][tb * 16 : (tb + 1) * 16], values[1][tb * 16 : (tb + 1) * 16], three], axis=0
            )
        for d in peers:
            if d:
                to = ypeer(d)
                send(vs.at[to], rv.at[NY - d], v_ss.at[d], v_rs.at[NY - d], g, x * NY + to)
            else:
                rv[0] = vs[y]

    r32 = lax.broadcasted_iota(jnp.int32, (32, SPAN), 0)
    l32 = lax.broadcasted_iota(jnp.int32, (32, SPAN), 1)
    pick = l32 == (r32 // 16) * span + (y // 2) * 16 + r32 % 16
    for d in (2, 6, 4, 1, 7, 3, 5):
        arrived(rv.at[d], v_rs.at[d])
    tops, totals = [], []
    for k in range(NY):
        three = rv[k, 32:48, :].astype(F32)
        tops.append(three[0:1] + three[1:2] + three[2:3])
        totals.append(three[3:4] + three[4:5] + three[5:6])
    peak = functools.reduce(jnp.maximum, tops)
    factors = [jnp.exp(t - peak) for t in tops]
    denom = functools.reduce(jnp.add, [f * t for f, t in zip(factors, totals)])
    shares = [
        jnp.sum(jnp.where(pick, f / denom, 0.0), axis=1, keepdims=True) for f in factors
    ]
    head = functools.reduce(
        jnp.add, [s * rv[k, :32, :].astype(F32) for k, s in enumerate(shares)]
    )
    ho[x, 0] = jnp.concatenate([head[:16], head[16:]], axis=1).astype(BF)

    def slot(r):
        return jnp.where(r < 5, jnp.maximum(2 * r - 1, 0), 2 * NY - 2 * r)

    STEPS = (0, 1, 7, 2, 6, 3, 5, 4)
    for d in FAR_Y:
        k = STEPS.index(NY - d)
        send(ho.at[x, 0], ho.at[x, k], y_ss.at[d], y_rs.at[k], g, x * NY + ypeer(d))
    for k in range(1, 5):
        arrived(ho.at[x, k], y_rs.at[k])
    for d in FAR_X:
        piece = ho.at[x, 0:5]
        send(piece, piece, x_ss.at[0, d], x_rs.at[0, d], g, xpeer(d) * NY + y)
    for k in range(5, 8):
        arrived(ho.at[x, k], y_rs.at[k])
    for d in FAR_X:
        piece = ho.at[x, 5:8]
        send(piece, piece, x_ss.at[1, d], x_rs.at[1, d], g, xpeer(d) * NY + y)

    for e in (0, 1, 3, 2):
        xx = xpeer(e)
        if e:
            arrived(ho.at[xx, 0:5], x_rs.at[0, NX - e])
            arrived(ho.at[xx, 5:8], x_rs.at[1, NX - e])
        lhs = jnp.concatenate(
            [
                jnp.concatenate(
                    [ho[xx, slot((2 * tb + hp - y) % NY)] for hp in range(2)], axis=1
                )
                for tb in range(4)
            ],
            axis=0,
        )
        part = dot_nt(lhs, wo[...]).astype(BF)
        for tb in range(4):
            to = 4 * xx + tb
            zs[to] = part[tb * 16 : (tb + 1) * 16]

            @pl.when(to != g)
            def _():
                remote(zs.at[to], z_out.at[g], z_ss.at[to], z_rs.at[g], to, inner).start()

    own = pltpu.make_async_copy(zs.at[g], z_out.at[g], z_ss.at[g])
    own.start()
    for d in range(1, NG):
        arrived(z_out.at[gpeer(d)], z_rs.at[gpeer(d)])
    own.wait()
    for d in range(1, NG):
        remote(zs.at[gpeer(d)], z_out.at[g], z_ss.at[gpeer(d)], z_rs.at[g], g, inner).wait_send()
    for copy in sends:
        copy.wait_send()


def local(q, ids, limits, latent, ka, va, kd, ku, vd, vu, wo):
    args = (
        q, ids.reshape(1, -1), limits, latent.T, ka, va, kd.swapaxes(2, 3), ku,
        vd.swapaxes(2, 3), vu, wo.T,
    )
    sem = pltpu.SemaphoreType.DMA
    v = pltpu.VMEM
    parts = pl.pallas_call(
        kernel,
        out_shape=jax.ShapeDtypeStruct((NG, 16, 256), BF),
        in_specs=[pl.BlockSpec(memory_space=pltpu.HBM)] * len(args),
        out_specs=pl.BlockSpec(memory_space=pltpu.HBM),
        scratch_shapes=[
            v(q.shape, BF),
            v((TOK * HEADS, NOPE), F32),
            v((TOK * HEADS, NOPE), F32),
            v((1, ids.shape[0]), jnp.int32),
            pltpu.SMEM(limits.shape, jnp.int32),
            v((NX, LAT + ROPE, SPAN), BF),
            v(ka.shape, BF),
            v(va.shape, BF),
            v(args[6].shape, BF),
            v(ku.shape, BF),
            v(args[8].shape, BF),
            v(vu.shape, BF),
            v((256, LAT), BF),
            v((NY, 48, 128), BF),
            v((2, 2 * NY * TOK, LAT + 128), BF),
            v((NY, 48, 128), BF),
            v((NY, 48, 128), BF),
            v((NX, NY, 16, 256), BF),
            v((NG, 16, 256), BF),
            sem((len(args),)),
            *[sem((NY,))] * 2,
            *[sem((NX,))] * 4,
            *[sem((NY,))] * 4,
            *[sem((2, NX))] * 2,
            *[sem((NG,))] * 2,
        ],
        compiler_params=pltpu.CompilerParams(
            collective_id=0, has_side_effects=True
        ),
    )(*args)
    return jnp.sum(parts.astype(F32), axis=0)[:, : wo.shape[1]].astype(BF)


def solution(mesh):
    in_specs = (
        P("inner", "grp", None),
        P(),
        P(),
        P("inner", None),
        P("grp", None, None),
        P("grp", None, None),
        P(None, "grp", None, None),
        P(None, "grp", None, None),
        P(None, "grp", None, None),
        P(None, "grp", None, None),
        P("grp", "inner"),
    )
    return jax.shard_map(
        local, mesh=mesh, in_specs=in_specs, out_specs=P("grp", "inner"), check_vma=False
    )
```

time: 47.6 us -> 43.3 us (0.910)
  the two profiles are of different devices: /device:TPU:1 before, /device:TPU:5 now
where the time goes in v2:
time: 43.3 us; the launch traced here: 43.1 us
  Pallas kernels  41.6 us (96%)
  other arithmetic  1.53 us (4%)
    pallas_call x1, Pallas kernels, local(): pl.pallas_call(kernel, out_shape=jax.ShapeDtypeStruct((NG, 16, 256), BF),...  41.6 us
    reduce_sum x1, other arithmetic, local(): return jnp.sum(parts.astype(F32), axis=0)[:, :wo.shape[1]].astype(BF)  1.53 us

profile of v2, /device:TPU:5, one launch (start us, length us, event | category | flops | bytes accessed | tf_op | source)
XLA Modules:
  0.0 43.1 jit_solution(900744715795640545)
XLA Ops:
  0.0 41.6 %shard_map.109 = bf16[16,16,256]{2,1,0:T(8,128)(2,1)} custom-call(bf16[8,4,192]{2,1,0:T(4,128)(2,1)} %q_hbm.1, s32[1,256]{1,0:T(1,128)} %bitcast.10, s32[4]{0:T(128)} %lim_hbm.1, bf16[576,128]{1,0:T(8,128)(2,1)} %bitcast.8, bf16[4,128,512]{2,1,0:T(8,128)(2,1)} %ka_hbm.1, bf16[4,512,128]{2,1,0:T(8,128)(2,1)} %va_hbm.1, bf16[4,4,16,128]{3,2,1,0:T(8,128)(2,1)} %bitcast.9, ...), custom_call_target="tpu_custom_call" | custom-call | tf_op jit(solution)/shard_map/pallas_call | solution.py:270
  41.6 1.5 %reduce = bf16[16,256]{1,0:T(8,128)(2,1)} reduce(bf16[16,16,256]{2,1,0:T(8,128)(2,1)} %shard_map.109, bf16[]{:T(256)} %constant.9), dimensions={0}, to_apply=%region_0.0.clone | reduce | flops 61440 | bytes 139266 | tf_op jit(solution)/shard_map/reduce_sum | solution.py:306

commit v3 on v2

--- a/solution.py
+++ b/solution.py
@@ -31,11 +31,13 @@
     z_out,
     q_v, q_n, q_r, ids_v, lim_s, lat, ka, va, kd, ku, vd, vu, wo,
     qbuf, qf, vs, rv, ho, zs,
-    lsem, q_ss, q_rs, l_ss, l_rs, c_ss, c_rs, v_ss, v_rs, y_ss, y_rs, x_ss, x_rs, z_ss, z_rs,
+    lsem, q_ss, q_rs, l_ss, l_rs, c_ss, c_rs, v_ss, v_rs, y_ss, y_rs, x_ss, x_rs, z_ss, z_rs, up_sem,
 ):
     g = lax.axis_index("grp")
     inner = lax.axis_index("inner")
     x, y = inner // NY, inner % NY
+    z = g // 2
+    core = 2 * z + 1 - g % 2
 
     def ypeer(d):
         return (y + d) % NY
@@ -74,8 +76,17 @@
         pl.semaphore_signal(barrier, 1, device_id=(g, x * NY + ypeer(d)), device_id_type=MESH)
     for d in FAR_X:
         pl.semaphore_signal(barrier, 1, device_id=(g, xpeer(d) * NY + y), device_id_type=MESH)
-    for d in range(1, NG):
-        pl.semaphore_signal(barrier, 1, device_id=(gpeer(d), inner), device_id_type=MESH)
+    pl.semaphore_signal(barrier, 1, device_id=(core, inner), device_id_type=MESH)
+    for k in range(NG):
+
+        @pl.when(k // 2 > z)
+        def _():
+            pl.semaphore_signal(barrier, 1, device_id=(k, inner), device_id_type=MESH)
+
+    pl.semaphore_wait(barrier, NY - 1 + NX - 1 + 1 + 2 * z)
+    part = pl.ds(pl.multiple_of((g % 2) * 288, 16), 288)
+    for d in FAR_X:
+        send(lat_hbm.at[part], lat.at[x, part], l_ss.at[d], l_rs.at[x], g, xpeer(d) * NY + y)
 
     get_q.wait()
     q32 = q_v[...].astype(F32)
@@ -86,16 +97,14 @@
     ropes = [q_r[pl.ds(h, TOK, stride=HEADS), :][:, :ROPE] for h in range(HEADS)]
     rows += [jnp.concatenate(ropes[h : h + 2], axis=1) for h in (0, 2)]
     qbuf[y] = jnp.concatenate(rows, axis=0).astype(BF)
-    get_lat.wait()
-
-    pl.semaphore_wait(barrier, NY - 1 + NX - 1 + NG - 1)
-
     for d in FAR_Y:
         send(qbuf.at[y], qbuf.at[y], q_ss.at[d], q_rs.at[y], g, x * NY + ypeer(d))
-    part = pl.ds(pl.multiple_of((g % 2) * 288, 16), 288)
-    for d in FAR_X:
-        piece = lat.at[x, part]
-        send(piece, piece, l_ss.at[d], l_rs.at[x], g, xpeer(d) * NY + y)
+    for k in range(NG):
+
+        @pl.when(k // 2 < z)
+        def _():
+            pl.semaphore_signal(up_sem, 1, device_id=(k, inner), device_id_type=MESH)
+
     get = [
         load(n + 2, src, dst)
         for n, (src, dst) in enumerate((
@@ -105,7 +114,7 @@
     ]
 
     wo[wo_hbm.shape[0] :, :] = jnp.zeros((wo.shape[0] - wo_hbm.shape[0], LAT), BF)
-    for copy in get:
+    for copy in [get_lat] + get:
         copy.wait()
     span = NY * TOK
     wide = NX * span
@@ -119,7 +128,6 @@
 
     for d in FAR_Y:
         arrived(qbuf.at[ypeer(d)], q_rs.at[ypeer(d)])
-    core = g + 1 - 2 * (g % 2)
     for d in (1, 3, 2):
         piece = lat.at[xpeer(d), part]
         arrived(piece, l_rs.at[xpeer(d)])
@@ -219,18 +227,24 @@
         arrived(ho.at[x, k], y_rs.at[k])
     for d in FAR_X:
         piece = ho.at[x, 0:5]
-        send(piece, piece, x_ss.at[0, d], x_rs.at[0, d], g, xpeer(d) * NY + y)
+        send(piece, piece, x_ss.at[0, d], x_rs.at[0, x], g, xpeer(d) * NY + y)
     for k in range(5, 8):
         arrived(ho.at[x, k], y_rs.at[k])
     for d in FAR_X:
         piece = ho.at[x, 5:8]
-        send(piece, piece, x_ss.at[1, d], x_rs.at[1, d], g, xpeer(d) * NY + y)
-
-    for e in (0, 1, 3, 2):
-        xx = xpeer(e)
-        if e:
-            arrived(ho.at[xx, 0:5], x_rs.at[0, NX - e])
-            arrived(ho.at[xx, 5:8], x_rs.at[1, NX - e])
+        send(piece, piece, x_ss.at[1, d], x_rs.at[1, x], g, xpeer(d) * NY + y)
+
+    @pl.when(z < NG // 2 - 1)
+    def _():
+        pl.semaphore_wait(up_sem, NG - 2 - 2 * z)
+
+    for xx in range(NX):
+
+        @pl.when(xx != x)
+        def _():
+            arrived(ho.at[xx, 0:5], x_rs.at[0, xx])
+            arrived(ho.at[xx, 5:8], x_rs.at[1, xx])
+
         lhs = jnp.concatenate(
             [
                 jnp.concatenate(
@@ -269,9 +283,9 @@
     v = pltpu.VMEM
     parts = pl.pallas_call(
         kernel,
-        out_shape=jax.ShapeDtypeStruct((NG, 16, 256), BF),
+        out_shape=pltpu.VMEM((NG, 16, 256), BF),
         in_specs=[pl.BlockSpec(memory_space=pltpu.HBM)] * len(args),
-        out_specs=pl.BlockSpec(memory_space=pltpu.HBM),
+        out_specs=pl.BlockSpec(memory_space=pltpu.VMEM),
         scratch_shapes=[
             v(q.shape, BF),
             v((TOK * HEADS, NOPE), F32),
@@ -298,6 +312,7 @@
             *[sem((NY,))] * 4,
             *[sem((2, NX))] * 2,
             *[sem((NG,))] * 2,
+            pltpu.SemaphoreType.REGULAR,
         ],
         compiler_params=pltpu.CompilerParams(
             collective_id=0, has_side_effects=True

time: 43.3 us -> 41.7 us (0.963)
  the two profiles are of different devices: /device:TPU:5 before, /device:TPU:3 now
where the time goes in v3:
time: 41.7 us; the launch traced here: 41.6 us
  Pallas kernels  40.9 us (98%)
  other arithmetic  0.62 us (1%)
    pallas_call x1, Pallas kernels, local(): pl.pallas_call(kernel, out_shape=pltpu.VMEM((NG, 16, 256), BF), in_specs=...  40.9 us

profile of v3, /device:TPU:3, one launch (start us, length us, event | category | flops | bytes accessed | tf_op | source)
XLA Modules:
  0.0 41.6 jit_solution(4942458723423316648)
XLA Ops:
  0.0 40.9 %shard_map.109 = bf16[16,16,256]{2,1,0:T(8,128)(2,1)S(1)} custom-call(bf16[8,4,192]{2,1,0:T(4,128)(2,1)} %q_hbm.1, s32[1,256]{1,0:T(1,128)} %bitcast.10, s32[4]{0:T(128)} %lim_hbm.1, bf16[576,128]{1,0:T(8,128)(2,1)} %bitcast.8, bf16[4,128,512]{2,1,0:T(8,128)(2,1)} %ka_hbm.1, bf16[4,512,128]{2,1,0:T(8,128)(2,1)} %va_hbm.1, bf16[4,4,16,128]{3,2,1,0:T(8,128)(2,1)} %bitcast.9, ...), custom_call_target="tpu_custom_call" | custom-call | tf_op jit(solution)/shard_map/pallas_call | solution.py:284
  40.9 0.6 %reduce = bf16[16,256]{1,0:T(8,128)(2,1)} reduce(bf16[16,16,256]{2,1,0:T(8,128)(2,1)S(1)} %shard_map.109, bf16[]{:T(256)} %constant.9), dimensions={0}, to_apply=%region_0.0.clone | reduce | flops 61440 | bytes 139266 | tf_op jit(solution)/shard_map/reduce_sum | solution.py:321

commit v4 on v3

--- a/solution.py
+++ b/solution.py
@@ -60,14 +60,10 @@
         return copy
 
     def arrived(dst, rs):
-        remote(dst, dst, q_ss.at[0], rs, g, inner).wait_recv()
-
-    sends = []
+        remote(dst, dst, q_ss, rs, g, inner).wait_recv()
 
     def send(*what):
-        copy = remote(*what)
-        copy.start()
-        sends.append(copy)
+        remote(*what).start()
 
     get_q = load(0, q_hbm, q_v)
     get_lat = load(1, lat_hbm, lat.at[x])
@@ -86,7 +82,7 @@
     pl.semaphore_wait(barrier, NY - 1 + NX - 1 + 1 + 2 * z)
     part = pl.ds(pl.multiple_of((g % 2) * 288, 16), 288)
     for d in FAR_X:
-        send(lat_hbm.at[part], lat.at[x, part], l_ss.at[d], l_rs.at[x], g, xpeer(d) * NY + y)
+        send(lat_hbm.at[part], lat.at[x, part], l_ss, l_rs.at[x], g, xpeer(d) * NY + y)
 
     get_q.wait()
     q32 = q_v[...].astype(F32)
@@ -98,7 +94,7 @@
     rows += [jnp.concatenate(ropes[h : h + 2], axis=1) for h in (0, 2)]
     qbuf[y] = jnp.concatenate(rows, axis=0).astype(BF)
     for d in FAR_Y:
-        send(qbuf.at[y], qbuf.at[y], q_ss.at[d], q_rs.at[y], g, x * NY + ypeer(d))
+        send(qbuf.at[y], qbuf.at[y], q_ss, q_rs, g, x * NY + ypeer(d))
     for k in range(NG):
 
         @pl.when(k // 2 < z)
@@ -126,12 +122,11 @@
         limit = jnp.where(tenant == k, lim_s[k], limit)
     chosen = lax.broadcasted_iota(jnp.int32, (span, 64), 1) // 16 == tenant
 
-    for d in FAR_Y:
-        arrived(qbuf.at[ypeer(d)], q_rs.at[ypeer(d)])
+    arrived(qbuf.at[: NY - 1], q_rs)
     for d in (1, 3, 2):
         piece = lat.at[xpeer(d), part]
         arrived(piece, l_rs.at[xpeer(d)])
-        send(piece, piece, c_ss.at[d], c_rs.at[d], core, inner)
+        send(piece, piece, c_ss, c_rs, core, inner)
 
     blocks = [qbuf[k].astype(F32) for k in range(NY)]
     half = lax.broadcasted_iota(jnp.int32, (span, NOPE), 1) // ROPE
@@ -147,8 +142,7 @@
         qf[h // 2, rows, LAT:] = jnp.where(half == h % 2, rope, 0.0).astype(BF)
 
     other = pl.ds(pl.multiple_of((1 - g % 2) * 288, 16), 288)
-    for d in (1, 3, 2):
-        arrived(lat.at[xpeer(d), other], c_rs.at[d])
+    arrived(lat.at[: NX - 1, other], c_rs)
 
     base = lax.broadcasted_iota(jnp.int32, (2 * span, SPAN), 1) + y * SPAN
     limit2 = jnp.concatenate([limit, limit], axis=0)
@@ -191,15 +185,14 @@
         for d in peers:
             if d:
                 to = ypeer(d)
-                send(vs.at[to], rv.at[NY - d], v_ss.at[d], v_rs.at[NY - d], g, x * NY + to)
+                send(vs.at[to], rv.at[NY - d], v_ss, v_rs, g, x * NY + to)
             else:
                 rv[0] = vs[y]
 
     r32 = lax.broadcasted_iota(jnp.int32, (32, SPAN), 0)
     l32 = lax.broadcasted_iota(jnp.int32, (32, SPAN), 1)
     pick = l32 == (r32 // 16) * span + (y // 2) * 16 + r32 % 16
-    for d in (2, 6, 4, 1, 7, 3, 5):
-        arrived(rv.at[d], v_rs.at[d])
+    arrived(rv.at[: NY - 1], v_rs)
     tops, totals = [], []
     for k in range(NY):
         three = rv[k, 32:48, :].astype(F32)
@@ -222,17 +215,15 @@
     STEPS = (0, 1, 7, 2, 6, 3, 5, 4)
     for d in FAR_Y:
         k = STEPS.index(NY - d)
-        send(ho.at[x, 0], ho.at[x, k], y_ss.at[d], y_rs.at[k], g, x * NY + ypeer(d))
-    for k in range(1, 5):
-        arrived(ho.at[x, k], y_rs.at[k])
+        send(ho.at[x, 0], ho.at[x, k], y_ss, y_rs.at[k // 5], g, x * NY + ypeer(d))
+    arrived(ho.at[x, 1:5], y_rs.at[0])
     for d in FAR_X:
         piece = ho.at[x, 0:5]
-        send(piece, piece, x_ss.at[0, d], x_rs.at[0, x], g, xpeer(d) * NY + y)
-    for k in range(5, 8):
-        arrived(ho.at[x, k], y_rs.at[k])
+        send(piece, piece, x_ss, x_rs.at[x], g, xpeer(d) * NY + y)
+    arrived(ho.at[x, 5:8], y_rs.at[1])
     for d in FAR_X:
         piece = ho.at[x, 5:8]
-        send(piece, piece, x_ss.at[1, d], x_rs.at[1, x], g, xpeer(d) * NY + y)
+        send(piece, piece, x_ss, x_rs.at[x], g, xpeer(d) * NY + y)
 
     @pl.when(z < NG // 2 - 1)
     def _():
@@ -242,8 +233,7 @@
 
         @pl.when(xx != x)
         def _():
-            arrived(ho.at[xx, 0:5], x_rs.at[0, xx])
-            arrived(ho.at[xx, 5:8], x_rs.at[1, xx])
+            arrived(ho.at[xx], x_rs.at[xx])
 
         lhs = jnp.concatenate(
             [
@@ -254,24 +244,23 @@
             ],
             axis=0,
         )
-        part = dot_nt(lhs, wo[...]).astype(BF)
+        share = dot_nt(lhs, wo[...]).astype(BF)
         for tb in range(4):
             to = 4 * xx + tb
-            zs[to] = part[tb * 16 : (tb + 1) * 16]
+            zs[to] = share[tb * 16 : (tb + 1) * 16]
 
             @pl.when(to != g)
             def _():
-                remote(zs.at[to], z_out.at[g], z_ss.at[to], z_rs.at[g], to, inner).start()
-
-    own = pltpu.make_async_copy(zs.at[g], z_out.at[g], z_ss.at[g])
-    own.start()
-    for d in range(1, NG):
-        arrived(z_out.at[gpeer(d)], z_rs.at[gpeer(d)])
-    own.wait()
-    for d in range(1, NG):
-        remote(zs.at[gpeer(d)], z_out.at[g], z_ss.at[gpeer(d)], z_rs.at[g], g, inner).wait_send()
-    for copy in sends:
-        copy.wait_send()
+                remote(zs.at[to], z_out.at[g], z_ss, z_rs, to, inner).start()
+
+    z_out[g] = zs[g]
+    arrived(z_out.at[: NG - 1], z_rs)
+    for sent, sem in (
+        (qbuf.at[: NY - 1], q_ss), (lat.at[: NX - 1, part], l_ss), (lat.at[: NX - 1, part], c_ss),
+        (rv.at[: NY - 1], v_ss), (ho.at[0, : NY - 1], y_ss), (ho.at[: NX - 1], x_ss),
+        (zs.at[: NG - 1], z_ss),
+    ):
+        remote(sent, sent, sem, q_rs, g, inner).wait_send()
 
 
 def local(q, ids, limits, latent, ka, va, kd, ku, vd, vu, wo):
@@ -307,11 +296,13 @@
             v((NX, NY, 16, 256), BF),
             v((NG, 16, 256), BF),
             sem((len(args),)),
-            *[sem((NY,))] * 2,
-            *[sem((NX,))] * 4,
-            *[sem((NY,))] * 4,
-            *[sem((2, NX))] * 2,
-            *[sem((NG,))] * 2,
+            *[sem] * 3,
+            sem((NX,)),
+            *[sem] * 5,
+            sem((2,)),
+            sem,
+            sem((NX,)),
+            *[sem] * 2,
             pltpu.SemaphoreType.REGULAR,
         ],
         compiler_params=pltpu.CompilerParams(

time: 41.7 us -> 40.8 us (0.978)
  Pallas kernels: 40.9 us -> 40 us
    pallas_call x1, Pallas kernels: 40.9 us -> 40 us  [local(): pl.pallas_call(kernel, out_shape=pltpu.VMEM((NG, 16, 256), BF), in_specs=...]
where the time goes in v4:
time: 40.8 us; the launch traced here: 40.7 us
  Pallas kernels  40 us (98%)
  other arithmetic  0.62 us (2%)
    pallas_call x1, Pallas kernels, local(): pl.pallas_call(kernel, out_shape=pltpu.VMEM((NG, 16, 256), BF), in_specs=...  40 us

profile of v4, /device:TPU:3, one launch (start us, length us, event | category | flops | bytes accessed | tf_op | source)
XLA Modules:
  0.0 40.7 jit_solution(18300942826920944301)
XLA Ops:
  0.0 40.0 %shard_map.109 = bf16[16,16,256]{2,1,0:T(8,128)(2,1)S(1)} custom-call(bf16[8,4,192]{2,1,0:T(4,128)(2,1)} %q_hbm.1, s32[1,256]{1,0:T(1,128)} %bitcast.10, s32[4]{0:T(128)} %lim_hbm.1, bf16[576,128]{1,0:T(8,128)(2,1)} %bitcast.8, bf16[4,128,512]{2,1,0:T(8,128)(2,1)} %ka_hbm.1, bf16[4,512,128]{2,1,0:T(8,128)(2,1)} %va_hbm.1, bf16[4,4,16,128]{3,2,1,0:T(8,128)(2,1)} %bitcast.9, ...), custom_call_target="tpu_custom_call" | custom-call | tf_op jit(solution)/shard_map/pallas_call | solution.py:273
  40.0 0.6 %reduce = bf16[16,256]{1,0:T(8,128)(2,1)} reduce(bf16[16,16,256]{2,1,0:T(8,128)(2,1)S(1)} %shard_map.109, bf16[]{:T(256)} %constant.9), dimensions={0}, to_apply=%region_0.0.clone | reduce | flops 61440 | bytes 139266 | tf_op jit(solution)/shard_map/reduce_sum | solution.py:312

commit v5 on v4

--- a/solution.py
+++ b/solution.py
@@ -73,11 +73,9 @@
     for d in FAR_X:
         pl.semaphore_signal(barrier, 1, device_id=(g, xpeer(d) * NY + y), device_id_type=MESH)
     pl.semaphore_signal(barrier, 1, device_id=(core, inner), device_id_type=MESH)
-    for k in range(NG):
-
-        @pl.when(k // 2 > z)
-        def _():
-            pl.semaphore_signal(barrier, 1, device_id=(k, inner), device_id_type=MESH)
+    @pl.loop(2 * z + 2, NG)
+    def _(k):
+        pl.semaphore_signal(barrier, 1, device_id=(k, inner), device_id_type=MESH)
 
     pl.semaphore_wait(barrier, NY - 1 + NX - 1 + 1 + 2 * z)
     part = pl.ds(pl.multiple_of((g % 2) * 288, 16), 288)
@@ -95,11 +93,9 @@
     qbuf[y] = jnp.concatenate(rows, axis=0).astype(BF)
     for d in FAR_Y:
         send(qbuf.at[y], qbuf.at[y], q_ss, q_rs, g, x * NY + ypeer(d))
-    for k in range(NG):
-
-        @pl.when(k // 2 < z)
-        def _():
-            pl.semaphore_signal(up_sem, 1, device_id=(k, inner), device_id_type=MESH)
+    @pl.loop(0, 2 * z)
+    def _(k):
+        pl.semaphore_signal(up_sem, 1, device_id=(k, inner), device_id_type=MESH)
 
     get = [
         load(n + 2, src, dst)
@@ -229,8 +225,8 @@
     def _():
         pl.semaphore_wait(up_sem, NG - 2 - 2 * z)
 
-    for xx in range(NX):
-
+    @pl.loop(0, NX)
+    def _(xx):
         @pl.when(xx != x)
         def _():
             arrived(ho.at[xx], x_rs.at[xx])

time: 40.8 us -> 40.7 us (level)
  no operation moved by 1% of the time
where the time goes in v5:
time: 40.7 us; the launch traced here: 40.5 us
  Pallas kernels  39.9 us (98%)
  other arithmetic  0.62 us (2%)
    pallas_call x1, Pallas kernels, local(): pl.pallas_call(kernel, out_shape=pltpu.VMEM((NG, 16, 256), BF), in_specs=...  39.9 us

profile of v5, /device:TPU:3, one launch (start us, length us, event | category | flops | bytes accessed | tf_op | source)
XLA Modules:
  0.0 40.5 jit_solution(799955535042341190)
XLA Ops:
  0.0 39.9 %shard_map.109 = bf16[16,16,256]{2,1,0:T(8,128)(2,1)S(1)} custom-call(bf16[8,4,192]{2,1,0:T(4,128)(2,1)} %q_hbm.1, s32[1,256]{1,0:T(1,128)} %bitcast.10, s32[4]{0:T(128)} %lim_hbm.1, bf16[576,128]{1,0:T(8,128)(2,1)} %bitcast.8, bf16[4,128,512]{2,1,0:T(8,128)(2,1)} %ka_hbm.1, bf16[4,512,128]{2,1,0:T(8,128)(2,1)} %va_hbm.1, bf16[4,4,16,128]{3,2,1,0:T(8,128)(2,1)} %bitcast.9, ...), custom_call_target="tpu_custom_call" | custom-call | tf_op jit(solution)/shard_map/pallas_call | solution.py:269
  39.9 0.6 %reduce = bf16[16,256]{1,0:T(8,128)(2,1)} reduce(bf16[16,16,256]{2,1,0:T(8,128)(2,1)S(1)} %shard_map.109, bf16[]{:T(256)} %constant.9), dimensions={0}, to_apply=%region_0.0.clone | reduce | flops 61440 | bytes 139266 | tf_op jit(solution)/shard_map/reduce_sum | solution.py:308

commit v6 on v5

--- a/solution.py
+++ b/solution.py
@@ -13,9 +13,10 @@
 NX, NY, NG = 4, 8, 16
 HEADS, TOK = 4, 8
 SPAN = 128
-MASKED = -30000.0
+LOG2E = 1.4426950408889634
+MASKED = -30000.0 * LOG2E
 FAR_Y, FAR_X = (4, 3, 5, 2, 6, 1, 7), (2, 1, 3)
-SCALE = (NOPE + ROPE) ** -0.5
+SCALE = (NOPE + ROPE) ** -0.5 * LOG2E
 
 
 def dot(a, b):
@@ -155,7 +156,7 @@
             scores.append(jnp.where(okay[b], dot(mine, keys) * SCALE, MASKED))
         top = functools.reduce(jnp.maximum, scores)
         top = jnp.max(top, axis=1, keepdims=True)
-        weights = [jnp.where(ok, jnp.exp(s - top), 0.0) for ok, s in zip(okay, scores)]
+        weights = [jnp.where(ok, jnp.exp2(s - top), 0.0) for ok, s in zip(okay, scores)]
         total = jnp.sum(functools.reduce(jnp.add, weights), axis=1, keepdims=True)
         acc = functools.reduce(
             jnp.add, [dot_nt(w.astype(BF), lat[b, :LAT]) for b, w in enumerate(weights)]
@@ -195,7 +196,7 @@
         tops.append(three[0:1] + three[1:2] + three[2:3])
         totals.append(three[3:4] + three[4:5] + three[5:6])
     peak = functools.reduce(jnp.maximum, tops)
-    factors = [jnp.exp(t - peak) for t in tops]
+    factors = [jnp.exp2(t - peak) for t in tops]
     denom = functools.reduce(jnp.add, [f * t for f, t in zip(factors, totals)])
     shares = [
         jnp.sum(jnp.where(pick, f / denom, 0.0), axis=1, keepdims=True) for f in factors

time: 40.7 us -> 40.7 us (level)
  no operation moved by 1% of the time
where the time goes in v6:
time: 40.7 us; the launch traced here: 40.5 us
  Pallas kernels  39.9 us (98%)
  other arithmetic  0.62 us (2%)
    pallas_call x1, Pallas kernels, local(): pl.pallas_call(kernel, out_shape=pltpu.VMEM((NG, 16, 256), BF), in_specs=...  39.9 us

profile of v6, /device:TPU:3, one launch (start us, length us, event | category | flops | bytes accessed | tf_op | source)
XLA Modules:
  0.0 40.5 jit_solution(16041920329643450555)
XLA Ops:
  0.0 39.9 %shard_map.109 = bf16[16,16,256]{2,1,0:T(8,128)(2,1)S(1)} custom-call(bf16[8,4,192]{2,1,0:T(4,128)(2,1)} %q_hbm.1, s32[1,256]{1,0:T(1,128)} %bitcast.10, s32[4]{0:T(128)} %lim_hbm.1, bf16[576,128]{1,0:T(8,128)(2,1)} %bitcast.8, bf16[4,128,512]{2,1,0:T(8,128)(2,1)} %ka_hbm.1, bf16[4,512,128]{2,1,0:T(8,128)(2,1)} %va_hbm.1, bf16[4,4,16,128]{3,2,1,0:T(8,128)(2,1)} %bitcast.9, ...), custom_call_target="tpu_custom_call" | custom-call | tf_op jit(solution)/shard_map/pallas_call | solution.py:270
  39.9 0.6 %reduce = bf16[16,256]{1,0:T(8,128)(2,1)} reduce(bf16[16,16,256]{2,1,0:T(8,128)(2,1)S(1)} %shard_map.109, bf16[]{:T(256)} %constant.9), dimensions={0}, to_apply=%region_0.0.clone | reduce | flops 61440 | bytes 139266 | tf_op jit(solution)/shard_map/reduce_sum | solution.py:309
